TPU v7x, 32 devices: a whole 2x2x4 slice. The times are simulated.
32 devices in a mesh: dp: 8 (over z, y), ctx: 4 (over x, core).
Axes of the slice: x: 2, y: 2, z: 4, core: 2. Of those that a mesh axis runs over, the one named last changes fastest.
Arguments:
- tokens: int32 [8, 512], P('dp', 'ctx'), may hold values from 0 to 511
- embedding: bfloat16 [512, 2048], replicated, may hold values from -6 to 6
- cotangent: bfloat16 [8, 512, 2048], P('dp', 'ctx'), may hold values from -6 to 6
- long_filter: float32 [128, 512], P('ctx'), may hold values from -1 to 1
- short_filter: float32 [3, 7, 2048], replicated, may hold values from -4 to 4
Outputs:
- block_output: bfloat16 [8, 512, 2048], P('dp', 'ctx')
- grad_input: bfloat16 [8, 512, 2048], P('dp', 'ctx')
- grad_long: float32 [128, 512], P('ctx')
- grad_short: float32 [3, 7, 2048], replicated
All inputs are finite; a program needn't handle non-finite values.
Results may differ from a plain program's by a relative error of at most 0.0058.
Values may be sent and summed in bfloat16 or wider, within the bound.
A program may use at most 64 MiB of HBM per device.

v0:
```python
import functools

import jax
import jax.numpy as jnp
from jax import lax
from jax.experimental import pallas as pl
from jax.experimental.pallas import tpu as pltpu
from jax.sharding import PartitionSpec as P

LANES = 128
F32 = jnp.float32
BF16 = jnp.bfloat16


def contract(a, b, da, db):
    return lax.dot_general(a, b, (((da,), (db,)), ((), ())), preferred_element_type=F32)


def kernel(taps, scale, tok_ref, emb_ref, cot_ref, h_ref, w_ref,
           blk_ref, gin_ref, long_ref, short_ref,
           hot, e_t, cot_t, blk_t, gin_t):
    vocab = emb_ref.shape[0]
    length, chans = cot_ref.shape
    groups = h_ref.shape[0]
    group = chans // groups
    n = length // LANES

    ids = lax.broadcasted_iota(jnp.int32, (vocab, length), 0)
    hot[...] = (ids == tok_ref[...]).astype(F32).astype(BF16)

    @pl.loop(0, chans // LANES)
    def _(c):
        cs = pl.ds(pl.multiple_of(c * LANES, LANES), LANES)
        e_t[cs, :] = contract(emb_ref[:, cs], hot[...], 0, 0)
        cot_t[cs, :] = cot_ref[:, cs].astype(F32).T

    @pl.loop(0, groups)
    def _(g):
        rows = pl.ds(pl.multiple_of(g * group, group), group)
        lane = lax.broadcasted_iota(jnp.int32, (group, length), 1)
        e = e_t[rows, :]
        es = [e] + [jnp.where(lane >= j, pltpu.roll(e, j, 1), 0.0) for j in range(1, taps)]
        w = w_ref[rows, :]
        col = [w[:, k:k + 1] for k in range(3 * taps)]

        def stream(s):
            total = col[s * taps] * es[0]
            for j in range(1, taps):
                total = total + col[s * taps + j] * es[j]
            return total

        q, k, v = stream(0), stream(1), stream(2)
        cot = cot_t[rows, :]
        x = (k * v).astype(BF16)
        gc = (cot * q).astype(BF16)
        xb = [x[:, i * LANES:(i + 1) * LANES] for i in range(n)]
        gb = [gc[:, i * LANES:(i + 1) * LANES] for i in range(n)]
        zero = jnp.zeros((group, LANES), BF16)
        lx = jnp.concatenate(
            [jnp.concatenate([xb[i - d] if d <= i else zero for d in range(n)], axis=1)
             for i in range(n)], axis=0)
        lg = jnp.concatenate(
            [jnp.concatenate([gb[i + d] if i + d < n else zero for d in range(n)], axis=1)
             for i in range(n)], axis=0)
        xs = jnp.concatenate(xb, axis=0)

        h = h_ref[pl.ds(g, 1), :]
        sub_i = lax.broadcasted_iota(jnp.int32, (LANES, LANES), 0)
        lane_i = lax.broadcasted_iota(jnp.int32, (LANES, LANES), 1)
        upper = lane_i >= sub_i
        prev = jnp.zeros((LANES, LANES), F32)
        ws = []
        for d in range(n):
            part = jnp.broadcast_to(h[:, d * LANES:(d + 1) * LANES], (LANES, LANES))
            turned = pltpu.roll(part, 0, 1, stride=1, stride_axis=0)
            ws.append(jnp.where(upper, turned, prev).astype(BF16))
            prev = turned
        conv = contract(lx, jnp.concatenate(ws, axis=0), 1, 0)
        gg = contract(lg, jnp.concatenate(ws, axis=1), 1, 1)
        cross = contract(xs, lg, 0, 0)

        def wide(a):
            return jnp.concatenate([a[i * group:(i + 1) * group] for i in range(n)], axis=1)

        cross = jnp.concatenate(
            [jnp.where(upper, cross[:, :LANES], 0.0), cross[:, LANES:]], axis=1)
        size = LANES
        while size > 8:
            size //= 2
            cross = cross[:size] + pltpu.roll(cross[size:], length - size, 1)
        while size > 1:
            size //= 2
            cross = cross + pltpu.roll(pltpu.roll(cross, 8 - size, 0), length - size, 1)
        long_ref[pl.ds(g, 1), :] = cross[0:1] * scale

        cb = wide(conv).astype(BF16).astype(F32)
        gb2 = wide(gg).astype(BF16).astype(F32)
        blk_t[rows, :] = q * cb
        grads = [cot * cb, gb2 * v, gb2 * k]
        total = None
        for j in range(taps - 1, -1, -1):
            term = (col[j] * grads[0] + col[taps + j] * grads[1]
                    + col[2 * taps + j] * grads[2])
            if total is not None:
                term = term + jnp.where(lane < length - 1, pltpu.roll(total, length - 1, 1), 0.0)
            total = term
        gin_t[rows, :] = total

        lane_k = lax.broadcasted_iota(jnp.int32, (group, LANES), 1)
        acc = jnp.zeros((group, LANES), F32)
        for s in range(3):
            for j in range(taps):
                prod = grads[s] * es[j]
                fold = prod[:, :LANES]
                for i in range(1, n):
                    fold = fold + prod[:, i * LANES:(i + 1) * LANES]
                acc = jnp.where(lane_k == s * taps + j, jnp.sum(fold, axis=1, keepdims=True), acc)
        short_ref[rows, :] = acc * scale

    @pl.loop(0, chans // LANES)
    def _(c):
        cs = pl.ds(pl.multiple_of(c * LANES, LANES), LANES)
        blk_ref[:, cs] = blk_t[cs, :].T.astype(BF16)
        gin_ref[:, cs] = gin_t[cs, :].T.astype(BF16)


def on_device(tokens, embedding, cotangent, long_filter, short_filter):
    streams, taps, channels = short_filter.shape
    vocab = embedding.shape[0]
    n_ctx = lax.axis_size("ctx")
    n_dp = lax.axis_size("dp")
    me = lax.axis_index("ctx")
    chans = channels // n_ctx
    groups, length = long_filter.shape
    scale = 1.0 / (n_dp * (chans // groups))

    ids = lax.all_gather(tokens, "ctx", axis=1, tiled=True)
    emb = lax.dynamic_slice(embedding, (0, me * chans), (vocab, chans))
    w = lax.dynamic_slice(short_filter.reshape(streams * taps, channels), (0, me * chans),
                          (streams * taps, chans))
    w = jnp.pad(w.T, ((0, 0), (0, LANES - streams * taps)))
    cot = lax.all_to_all(cotangent, "ctx", split_axis=2, concat_axis=1, tiled=True)[0]
    vmem = pl.BlockSpec(memory_space=pltpu.VMEM)
    blk, gin, long_part, short_part = pl.pallas_call(
        functools.partial(kernel, taps, scale),
        out_shape=[
            jax.ShapeDtypeStruct((length, chans), BF16),
            jax.ShapeDtypeStruct((length, chans), BF16),
            jax.ShapeDtypeStruct((groups, length), F32),
            jax.ShapeDtypeStruct((chans, LANES), F32),
        ],
        in_specs=[vmem] * 5,
        out_specs=[vmem] * 4,
        scratch_shapes=[
            pltpu.VMEM((vocab, length), BF16),
            pltpu.VMEM((chans, length), F32),
            pltpu.VMEM((chans, length), F32),
            pltpu.VMEM((chans, length), F32),
            pltpu.VMEM((chans, length), F32),
        ],
        compiler_params=pltpu.CompilerParams(vmem_limit_bytes=48 * 1024 * 1024),
        name="hyena",
    )(ids, emb, cot, long_filter, w)
    both = jnp.stack([blk, gin])
    both = lax.all_to_all(both, "ctx", split_axis=1, concat_axis=2, tiled=True)
    grad_long = lax.psum(long_part, "dp")
    short_part = short_part[:, :streams * taps].T
    short_sum = lax.psum(short_part, "dp")
    grad_short = lax.all_gather(short_sum, "ctx", axis=1, tiled=True)
    return (both[0:1], both[1:2], grad_long, grad_short.reshape(streams, taps, channels))


def solution(mesh):
    in_specs = (P("dp", "ctx"), P(), P("dp", "ctx", None), P("ctx", None), P())
    out_specs = (P("dp", "ctx", None), P("dp", "ctx", None), P("ctx", None), P())
    return jax.shard_map(
        on_device, mesh=mesh, in_specs=in_specs, out_specs=out_specs, check_vma=False
    )
```

profile of v0, /device:TPU:0, one launch (start us, length us, event | category | flops | bytes accessed | tf_op | source)
XLA Modules:
  0.0 170.4 jit_solution(15225177176309072600)
XLA Ops:
  7.2 2.5 %copy.26 = bf16[1,128,2048]{1,0,2:T(2,128)(2,1)S(1)} copy(bf16[1,128,2048]{2,1,0:T(8,128)(2,1)} %param.7) | data formatting | bytes 1048576 | tf_op args[2]
  10.2 12.3 %reduce = bf16[2048,128]{1,0:T(8,128)(2,1)} reduce(bf16[2048,1,128]{2,1,0:T(2,128)(2,1)S(1)} %bitcast.19, bf16[]{:T(256)} %broadcast.2), dimensions={1}, to_apply=%bitcast.12.reduce_sub_computation | reduce | bytes 1048578
  22.5 2.0 %reshape.19 = bf16[4,2,32768]{2,1,0:T(2,128)(2,1)} reshape(bf16[2048,128]{1,0:T(8,128)(2,1)} %reduce) | data formatting | bytes 1048576
  24.5 4.2 %all-to-all-start = ((bf16[4,2,32768]{2,1,0:T(2,128)(2,1)}), bf16[4,2,32768]{2,1,0:T(2,128)(2,1)S(1)}, u32[]{:S(2)}, u32[]{:S(2)}) async-start(bf16[4,2,32768]{2,1,0:T(2,128)(2,1)} %reshape.19), calls=%async_computation | async-start | bytes 1048576 | tf_op jit(solution)/shard_map/all_to_all | solution.py:142
  28.9 9.5 %all_gather.6.tok_ref = s32[1,512]{1,0:T(1,128)S(1)} all-gather(s32[1,128]{1,0:T(1,128)S(1)} %copy-done.6), channel_id=1, replica_groups=mesh['dp'=8,'ctx'=4] {'ctx'}, dimensions={1}, use_global_device_ids=true | all-gather | bytes 2560 | tf_op jit(solution)/shard_map/all_gather | solution.py:137
  38.5 1.8 %reshape.20 = bf16[2048,1,128]{2,1,0:T(2,128)(2,1)} reshape(bf16[4,2,32768]{2,1,0:T(2,128)(2,1)S(1)} %all-to-all-done) | data formatting | bytes 1048576
  40.3 2.1 %copy.33 = bf16[1,128,2048]{1,2,0:T(8,128)(2,1)} copy(bf16[1,128,2048]{1,0,2:T(2,128)(2,1)} %bitcast.18) | data formatting | bytes 1048576
  42.4 1.2 copy.27
  43.6 36.2 %hyena.1 = (bf16[512,512]{1,0:T(8,128)(2,1)S(1)}, bf16[512,512]{1,0:T(8,128)(2,1)S(1)}, f32[32,512]{1,0:T(8,128)}, f32[512,128]{1,0:T(8,128)S(1)}) custom-call(s32[1,512]{1,0:T(1,128)S(1)} %all_gather.6.tok_ref, bf16[512,512]{1,0:T(8,128)(2,1)S(1)} %constant_dynamic-slice_fusion.1.emb_ref, bf16[512,512]{1,0:T(8,128)(2,1)S(1)} %bitcast.14, ...), custom_call_target="tpu_custom_call" | custom-call | tf_op jit(solution)/shard_map/hyena/pallas_call | solution.py:144
  80.5 2.0 %copy.29 = bf16[2,512,512]{2,0,1:T(2,128)(2,1)} copy(bf16[2,512,512]{2,1,0:T(8,128)(2,1)S(1)} %pad_maximum_fusion) | data formatting | bytes 2097152 | tf_op jit(solution)/shard_map/stack | solution.py:164
  82.5 3.6 %all-to-all-start.1 = ((bf16[2,512,512]{2,0,1:T(2,128)(2,1)}), bf16[2,512,512]{2,0,1:T(2,128)(2,1)S(1)}, u32[]{:S(2)}, u32[]{:S(2)}) async-start(bf16[2,512,512]{2,0,1:T(2,128)(2,1)} %copy.29), calls=%async_computation.1 | async-start | bytes 2097152 | tf_op jit(solution)/shard_map/all_to_all | solution.py:165
  86.3 0.7 all-reduce.3.cloned.1.call-update
  87.0 0.7 slice_bitcast_fusion
  87.7 41.8 %psum.15 = f32[21,512]{0,1:T(8,128)S(1)} all-reduce(f32[21,512]{0,1:T(8,128)} %slice_bitcast_fusion), channel_id=1, replica_groups=mesh['dp'=8,'ctx'=4] {'dp'}, use_global_device_ids=true, to_apply=%region_1.2 | all-reduce | flops 10752 | bytes 86016 | tf_op jit(solution)/shard_map/psum | solution.py:168
  129.4 11.4 %all_gather.7 = f32[21,2048]{0,1:T(8,128)} all-gather(f32[21,512]{0,1:T(8,128)S(1)} %psum.15), channel_id=1, replica_groups=mesh['dp'=8,'ctx'=4] {'ctx'}, dimensions={1}, use_global_device_ids=true | all-gather | bytes 215040 | tf_op jit(solution)/shard_map/all_gather | solution.py:169
  140.8 1.6 copy.32
  142.4 0.7 reshape.18
  143.1 2.3 %fusion = (bf16[1,128,4,512]{3,0,1,2:T(2,128)(2,1)S(1)}, bf16[1,128,4,512]{3,0,1,2:T(2,128)(2,1)}) fusion(bf16[2,128,4,512]{3,0,1,2:T(2,128)(2,1)S(1)} %bitcast.17), kind=kLoop, calls=%fused_computation.4 | loop fusion | bytes 2097152 | tf_op jit(solution)/shard_map/slice | solution.py:170
  145.3 1.5 copy.31
  146.8 2.2 %slice.18 = bf16[1,128,2048]{2,1,0:T(8,128)(2,1)} reshape(bf16[1,128,4,512]{3,2,1,0:T(4,128)(2,1)} %copy.31) | data formatting | bytes 1048576 | tf_op jit(solution)/shard_map/slice | solution.py:170
  149.0 1.5 copy.30
  150.5 2.2 %slice.16 = bf16[1,128,2048]{2,1,0:T(8,128)(2,1)} reshape(bf16[1,128,4,512]{3,2,1,0:T(4,128)(2,1)} %copy.30) | data formatting | bytes 1048576 | tf_op jit(solution)/shard_map/slice | solution.py:170
  152.7 9.4 %all-reduce.3.cloned.1.call-done = f32[32,512]{1,0:T(8,128)} async-done(((f32[32,512]{1,0:T(8,128)}), f32[32,512]{1,0:T(8,128)}) %all-reduce.3.cloned.1.call-update) | async-done | bytes 65552 | tf_op jit(solution)/shard_map/psum | solution.py:166
  162.1 1.5 copy.36
  (24 shorter events, 1.5 us)
Async XLA Ops:
  7.2 31.3 %copy-start = (bf16[512,2048]{1,0:T(8,128)(2,1)S(1)}, bf16[512,2048]{1,0:T(8,128)(2,1)}, u32[]{:S(2)}) copy-start(bf16[512,2048]{1,0:T(8,128)(2,1)} %param.6) | copy-start | bytes 6291460
  9.7 19.0 %copy-start.5 = (f32[3,7,2048]{2,1,0:T(8,128)S(1)}, f32[3,7,2048]{2,1,0:T(8,128)}, u32[]{:S(2)}) copy-start(f32[3,7,2048]{2,1,0:T(8,128)} %param.9) | copy-start | bytes 516100
  22.5 6.4 %copy-start.6 = (s32[1,128]{1,0:T(1,128)S(1)}, s32[1,128]{1,0:T(1,128)}, u32[]{:S(2)}) copy-start(s32[1,128]{1,0:T(1,128)} %param.5) | copy-start | bytes 1540
  24.5 14.0 %all-to-all-start = ((bf16[4,2,32768]{2,1,0:T(2,128)(2,1)}), bf16[4,2,32768]{2,1,0:T(2,128)(2,1)S(1)}, u32[]{:S(2)}, u32[]{:S(2)}) async-start(bf16[4,2,32768]{2,1,0:T(2,128)(2,1)} %reshape.19), calls=%async_computation | async-start | bytes 1048576 | tf_op jit(solution)/shard_map/all_to_all | solution.py:142
  38.5 5.1 %copy-start.3 = (f32[32,512]{1,0:T(8,128)S(1)}, f32[32,512]{1,0:T(8,128)}, u32[]{:S(2)}) copy-start(f32[32,512]{1,0:T(8,128)} %h_ref.1) | copy-start | bytes 196612
  79.8 0.7 copy-start.1
  82.5 4.4 %copy-start.2 = (f32[512,128]{1,0:T(8,128)S(1)}, f32[512,128]{1,0:T(8,128)}, u32[]{:S(2)}) copy-start(f32[512,128]{1,0:T(8,128)} %copy-done.1) | copy-start | bytes 786436
  82.5 60.5 %all-to-all-start.1 = ((bf16[2,512,512]{2,0,1:T(2,128)(2,1)}), bf16[2,512,512]{2,0,1:T(2,128)(2,1)S(1)}, u32[]{:S(2)}, u32[]{:S(2)}) async-start(bf16[2,512,512]{2,0,1:T(2,128)(2,1)} %copy.29), calls=%async_computation.1 | async-start | bytes 2097152 | tf_op jit(solution)/shard_map/all_to_all | solution.py:165
  86.2 75.9 %all-reduce.3.cloned.1.call-start = ((), (), s32[]{:S(2)}) async-start(), calls=%async_computation.2 | async-start | bytes 131072 | tf_op jit(solution)/shard_map/psum | solution.py:166
  145.3 3.7 %copy-start.4 = (bf16[1,128,4,512]{3,0,1,2:T(2,128)(2,1)S(1)}, bf16[1,128,4,512]{3,0,1,2:T(2,128)(2,1)}, u32[]{:S(2)}) copy-start(bf16[1,128,4,512]{3,0,1,2:T(2,128)(2,1)} %get-tuple-element.17) | copy-start | bytes 1572868
Sparse Core Ops, SparseCore 0:
  91.0 70.9 all-reduce.2
where the time goes:
time: 171 us; the launch traced here: 170 us
  blocking collectives  62.6 us (37%)
  Pallas kernels  36.2 us (21%)
  local copies, waits for them, and re-layouts  27.1 us (16%)
  between operations  14.2 us (8%)
  other arithmetic  12.4 us (7%)
  waiting for transfers between devices  10.1 us (6%)
  starting transfers between devices  7.9 us (5%)
    psum x1, blocking collectives, on_device(): short_sum = lax.psum(short_part, 'dp')  41.8 us
    pallas_call x1, Pallas kernels, on_device(): pl.pallas_call(functools.partial(kernel, taps, scale), out_shape=[jax.Sha...  36.2 us
    unnamed x1, other arithmetic  12.3 us
    all_gather x1, blocking collectives, on_device(): grad_short = lax.all_gather(short_sum, 'ctx', axis=1, tiled=True)  11.4 us
    unnamed x21, local copies, waits for them, and re-layouts  11.1 us
    all_gather x1, blocking collectives, on_device(): ids = lax.all_gather(tokens, 'ctx', axis=1, tiled=True)  9.5 us
    psum x1, waiting for transfers between devices, on_device(): grad_long = lax.psum(long_part, 'dp')  9.38 us
    slice x3, local copies, waits for them, and re-layouts, on_device(): both[1:2]  5.93 us
  transfers between devices with their start and end apart: 3, of which 1 were waited for; matrix products, arithmetic and copies ran while one was open for 8% of the time, Pallas kernels for 0%

commit v1 on v0

v1 whole, which is shorter than its diff:
```python
import jax
import jax.numpy as jnp
from jax import lax
from jax.experimental import pallas as pl
from jax.experimental.pallas import tpu as pltpu
from jax.sharding import PartitionSpec as P

LANES = 128
F32 = jnp.float32
BF16 = jnp.bfloat16
MESH = pl.DeviceIdType.MESH


def contract(a, b, da, db):
    return lax.dot_general(a, b, (((da,), (db,)), ((), ())), preferred_element_type=F32)


def kernel(tok_ref, emb_ref, cot_ref, h_ref, w_ref,
           blk_ref, gin_ref, long_ref, short_ref,
           ids, emb, cot_b, hot, e_t, cot_t, blk_t, gin_t, w_s, w_t, blk_s, gin_s,
           long_s, short_t, red, got, summed, short_b,
           emb_sem, own_sem, out_sem, tok_send, tok_recv, cot_send, cot_recv,
           res_send, res_recv, red_send, red_recv, sum_send, sum_recv, sh_send, sh_recv):
    n_ctx, n_dp = lax.axis_size("ctx"), lax.axis_size("dp")
    me, mine = lax.axis_index("ctx"), lax.axis_index("dp")
    vocab, chans = emb.shape
    taps = w_ref.shape[1]
    groups, length = h_ref.shape
    group = chans // groups
    n = length // LANES
    own_len = tok_ref.shape[1]
    chunks = chans // LANES
    scale = 1.0 / (n_dp * group)
    per = got.shape[1]
    where = pl.ds(pl.multiple_of(me * chans, chans), chans)

    def ctx(k):
        return lax.rem(me + k, n_ctx)

    def dp(k):
        return lax.rem(mine + k, n_dp)

    def remote(src, dst, send, recv, target):
        return pltpu.make_async_remote_copy(
            src_ref=src, dst_ref=dst, send_sem=send, recv_sem=recv,
            device_id=target, device_id_type=MESH)

    emb_copy = pltpu.make_async_copy(emb_ref.at[:, where], emb, emb_sem)
    emb_copy.start()

    def cot_part(p, c):
        return cot_ref.at[0, :, pl.ds(pl.multiple_of(p * chans + c * LANES, LANES), LANES)]

    def own_cot(c):
        return pltpu.make_async_copy(cot_part(me, c), cot_b.at[c, me], own_sem.at[c])

    for c in range(chunks):
        own_cot(c).start()

    barrier = pltpu.get_barrier_semaphore()
    for k in range(1, n_ctx):
        pl.semaphore_signal(barrier, inc=1, device_id={"ctx": ctx(k)}, device_id_type=MESH)

    @pl.loop(1, n_dp)
    def _(k):
        pl.semaphore_signal(barrier, inc=1, device_id={"dp": dp(k)}, device_id_type=MESH)

    pl.semaphore_wait(barrier, n_ctx + n_dp - 2)

    def tok_copy(k, slot):
        return remote(tok_ref, ids.at[slot], tok_send.at[k], tok_recv.at[k], {"ctx": ctx(k)})

    def cot_copy(k, c, slot):
        return remote(cot_part(ctx(k), c), cot_b.at[c, slot],
                      cot_send.at[c, k], cot_recv.at[c, k], {"ctx": ctx(k)})

    for k in range(1, n_ctx):
        tok_copy(k, me).start()
    for c in range(chunks):
        for k in range(1, n_ctx):
            cot_copy(k, c, me).start()
    ids[me] = tok_ref[...]

    w_s[...] = jnp.zeros_like(w_s)
    for s in range(3):
        w_s[s * 8:s * 8 + taps, :] = w_ref[s, :, where]
    for c in range(chunks):
        w_t[c * LANES:(c + 1) * LANES, :] = w_s[:, c * LANES:(c + 1) * LANES].T
    if red.shape[0] > (groups // 8) * n + 3 * chunks:
        red[...] = jnp.zeros_like(red)

    for k in range(1, n_ctx):
        tok_copy(k, ctx(n_ctx - k)).wait()
    rows_v = lax.broadcasted_iota(jnp.int32, (vocab, own_len), 0)
    for i in range(n_ctx):
        hot[:, i * own_len:(i + 1) * own_len] = (rows_v == ids[i]).astype(F32).astype(BF16)
    emb_copy.wait()

    sub_i = lax.broadcasted_iota(jnp.int32, (LANES, LANES), 0)
    lane_i = lax.broadcasted_iota(jnp.int32, (LANES, LANES), 1)
    upper = lane_i >= sub_i
    lane = lax.broadcasted_iota(jnp.int32, (group, length), 1)
    lane_k = lax.broadcasted_iota(jnp.int32, (group, LANES), 1)

    def first(g):
        rows = pl.ds(pl.multiple_of(g * group, group), group)
        e = e_t[rows, :]
        es = [e] + [jnp.where(lane >= j, pltpu.roll(e, j, 1), 0.0) for j in range(1, taps)]
        w = w_t[rows, :]
        col = [[w[:, s * 8 + j:s * 8 + j + 1] for j in range(taps)] for s in range(3)]

        def stream(s):
            total = col[s][0] * es[0]
            for j in range(1, taps):
                total = total + col[s][j] * es[j]
            return total

        q, k, v = stream(0), stream(1), stream(2)
        cot = cot_t[rows, :]
        x = (k * v).astype(BF16)
        gc = (cot * q).astype(BF16)
        return rows, es, col, q, k, v, cot, x, gc

    def second(g, x, gc):
        xb = [x[:, i * LANES:(i + 1) * LANES] for i in range(n)]
        gb = [gc[:, i * LANES:(i + 1) * LANES] for i in range(n)]
        zero = jnp.zeros((group, LANES), BF16)
        lx = jnp.concatenate(
            [jnp.concatenate([xb[i - d] if d <= i else zero for d in range(n)], axis=1)
             for i in range(n)], axis=0)
        lg = jnp.concatenate(
            [jnp.concatenate([gb[i + d] if i + d < n else zero for d in range(n)], axis=1)
             for i in range(n)], axis=0)
        xs = jnp.concatenate(xb, axis=0)
        h = h_ref[pl.ds(g, 1), :]
        prev = jnp.zeros((LANES, LANES), F32)
        ws = []
        for d in range(n):
            part = jnp.broadcast_to(h[:, d * LANES:(d + 1) * LANES], (8, LANES))
            base = pltpu.roll(part, 0, 1, stride=1, stride_axis=0)
            turned = jnp.concatenate(
                [base] + [pltpu.roll(base, m, 1) for m in range(8, LANES, 8)], axis=0)
            ws.append(jnp.where(upper, turned, prev).astype(BF16))
            prev = turned
        conv = contract(lx, jnp.concatenate(ws, axis=0), 1, 0)
        gg = contract(lg, jnp.concatenate(ws, axis=1), 1, 1)
        cross = contract(xs, lg, 0, 0)
        return conv, gg, cross

    def wide(a):
        return jnp.concatenate([a[i * group:(i + 1) * group] for i in range(n)], axis=1)

    def third(g, rows, es, col, q, k, v, cot, conv, gg, cross):
        cross = jnp.concatenate(
            [jnp.where(upper, cross[:, :LANES], 0.0), cross[:, LANES:]], axis=1)
        size = LANES
        while size > 8:
            size //= 2
            cross = cross[:size] + pltpu.roll(cross[size:], length - size, 1)
        while size > 1:
            size //= 2
            cross = cross + pltpu.roll(pltpu.roll(cross, 8 - size, 0), length - size, 1)
        long_s[pl.ds(g, 1), :] = cross[0:1] * scale

        cb = wide(conv).astype(BF16).astype(F32)
        gb2 = wide(gg).astype(BF16).astype(F32)
        blk_t[rows, :] = q * cb
        grads = [cot * cb, gb2 * v, gb2 * k]
        total = None
        for j in range(taps - 1, -1, -1):
            term = col[0][j] * grads[0] + col[1][j] * grads[1] + col[2][j] * grads[2]
            if total is not None:
                term = term + jnp.where(lane < length - 1, pltpu.roll(total, length - 1, 1), 0.0)
            total = term
        gin_t[rows, :] = total
        acc = jnp.zeros((group, LANES), F32)
        for s in range(3):
            for j in range(taps):
                prod = grads[s] * es[j]
                fold = prod[:, :LANES]
                for i in range(1, n):
                    fold = fold + prod[:, i * LANES:(i + 1) * LANES]
                acc = jnp.where(lane_k == s * 8 + j, jnp.sum(fold, axis=1, keepdims=True), acc)
        short_t[rows, :] = acc * scale

    def results(c, k):
        at = pl.ds(pl.multiple_of(me * chans + c * LANES, LANES), LANES)
        to = ctx(k)
        return [remote(src.at[c, to], dst.at[0, :, at], res_send.at[i, c, k],
                       res_recv.at[i, c, k], {"ctx": to})
                for i, (src, dst) in enumerate(((blk_s, blk_ref), (gin_s, gin_ref)))]

    def arrivals(c, k):
        src_dev = ctx(n_ctx - k)
        at = pl.ds(pl.multiple_of(src_dev * chans + c * LANES, LANES), LANES)
        return [remote(src.at[c, me], dst.at[0, :, at], res_send.at[i, c, k],
                       res_recv.at[i, c, k], {"ctx": ctx(k)})
                for i, (src, dst) in enumerate(((blk_s, blk_ref), (gin_s, gin_ref)))]

    def own_results(c):
        at = pl.ds(pl.multiple_of(me * chans + c * LANES, LANES), LANES)
        return [pltpu.make_async_copy(src.at[c, me], dst.at[0, :, at], out_sem.at[i, c])
                for i, (src, dst) in enumerate(((blk_s, blk_ref), (gin_s, gin_ref)))]

    in_chunk = LANES // group
    step = 2 if in_chunk % 2 == 0 else 1

    @pl.loop(0, chunks)
    def _(c):
        cs = pl.ds(pl.multiple_of(c * LANES, LANES), LANES)
        e_t[cs, :] = contract(emb[:, cs], hot[...], 0, 0)
        own_cot(c).wait()
        for k in range(1, n_ctx):
            cot_copy(k, c, ctx(n_ctx - k)).wait()
        for i in range(n_ctx):
            cot_t[cs, i * own_len:(i + 1) * own_len] = cot_b[c, i].astype(F32).T

        @pl.loop(0, in_chunk // step)
        def _(i):
            gs = [c * in_chunk + i * step + u for u in range(step)]
            a = [first(g) for g in gs]
            m = [second(g, r[7], r[8]) for g, r in zip(gs, a)]
            for g, r, z in zip(gs, a, m):
                third(g, *r[:7], *z)

        for i in range(n_ctx):
            blk_s[c, i] = blk_t[cs, i * own_len:(i + 1) * own_len].T.astype(BF16)
            gin_s[c, i] = gin_t[cs, i * own_len:(i + 1) * own_len].T.astype(BF16)
        for k in range(1, n_ctx):
            for copy in results(c, k):
                copy.start()
        for copy in own_results(c):
            copy.start()

    t = 0
    for r in range(groups // 8):
        for i in range(n):
            red[t] = long_s[r * 8:(r + 1) * 8, i * LANES:(i + 1) * LANES]
            t += 1
    for c in range(chunks):
        turned = short_t[c * LANES:(c + 1) * LANES, :].T
        for r in range(3):
            red[t] = turned[r * 8:(r + 1) * 8, :]
            t += 1

    def part_copy(k, slot):
        return remote(red.at[pl.ds(dp(k) * per, per)], got.at[slot],
                      red_send.at[k], red_recv.at[k], {"dp": dp(k)})

    def sum_copy(k, slot):
        return remote(summed.at[mine], summed.at[slot],
                      sum_send.at[k], sum_recv.at[k], {"dp": dp(k)})

    for k in range(1, n_dp):
        part_copy(k, mine).start()
    got[mine] = red[pl.ds(mine * per, per)]
    for k in range(1, n_dp):
        part_copy(k, dp(n_dp - k)).wait()
    total = got[0]
    for i in range(1, n_dp):
        total = total + got[i]
    summed[mine] = total
    for k in range(1, n_dp):
        sum_copy(k, mine).start()
    for k in range(1, n_dp):
        sum_copy(k, dp(n_dp - k)).wait()

    base_t = (groups // 8) * n
    for c in range(chunks):
        for r in range(3):
            t = base_t + c * 3 + r
            short_b[me, r, :, c * LANES:(c + 1) * LANES] = summed[t // per, t % per]

    def short_copy(k, slot):
        return remote(short_b.at[me], short_b.at[slot],
                      sh_send.at[k], sh_recv.at[k], {"ctx": ctx(k)})

    for k in range(1, n_ctx):
        short_copy(k, me).start()
    t = 0
    for r in range(groups // 8):
        for i in range(n):
            long_ref[r * 8:(r + 1) * 8, i * LANES:(i + 1) * LANES] = summed[t // per, t % per]
            t += 1
    for k in range(1, n_ctx):
        short_copy(k, ctx(n_ctx - k)).wait()
    for i in range(n_ctx):
        for s in range(3):
            short_ref[s, :, i * chans:(i + 1) * chans] = short_b[i, s, :taps, :]

    @pl.loop(0, chunks)
    def _(c):
        for k in range(1, n_ctx):
            for copy in arrivals(c, k):
                copy.wait()
        for copy in own_results(c):
            copy.wait()


def on_device(tokens, embedding, cotangent, long_filter, short_filter):
    streams, taps, channels = short_filter.shape
    vocab = embedding.shape[0]
    n_ctx = lax.axis_size("ctx")
    n_dp = lax.axis_size("dp")
    chans = channels // n_ctx
    groups, length = long_filter.shape
    own_len = cotangent.shape[1]
    chunks = chans // LANES
    tiles = (groups // 8) * (length // LANES) + streams * chunks
    per = -(-tiles // n_dp)
    vmem = pl.BlockSpec(memory_space=pltpu.VMEM)
    hbm = pl.BlockSpec(memory_space=pl.ANY)
    dma = pltpu.SemaphoreType.DMA
    return pl.pallas_call(
        kernel,
        out_shape=[
            jax.ShapeDtypeStruct(cotangent.shape, BF16),
            jax.ShapeDtypeStruct(cotangent.shape, BF16),
            jax.ShapeDtypeStruct((groups, length), F32),
            jax.ShapeDtypeStruct(short_filter.shape, F32),
        ],
        in_specs=[vmem, hbm, hbm, vmem, vmem],
        out_specs=[hbm, hbm, vmem, vmem],
        scratch_shapes=[
            pltpu.VMEM((n_ctx, 1, own_len), jnp.int32),
            pltpu.VMEM((vocab, chans), BF16),
            pltpu.VMEM((chunks, n_ctx, own_len, LANES), BF16),
            pltpu.VMEM((vocab, length), BF16),
            pltpu.VMEM((chans, length), F32),
            pltpu.VMEM((chans, length), F32),
            pltpu.VMEM((chans, length), F32),
            pltpu.VMEM((chans, length), F32),
            pltpu.VMEM((LANES, chans), F32),
            pltpu.VMEM((chans, LANES), F32),
            pltpu.VMEM((chunks, n_ctx, own_len, LANES), BF16),
            pltpu.VMEM((chunks, n_ctx, own_len, LANES), BF16),
            pltpu.VMEM((groups, length), F32),
            pltpu.VMEM((chans, LANES), F32),
            pltpu.VMEM((per * n_dp, 8, LANES), F32),
            pltpu.VMEM((n_dp, per, 8, LANES), F32),
            pltpu.VMEM((n_dp, per, 8, LANES), F32),
            pltpu.VMEM((n_ctx, streams, 8, chans), F32),
            dma, dma((chunks,)), dma((2, chunks)),
            dma((n_ctx,)), dma((n_ctx,)),
            dma((chunks, n_ctx)), dma((chunks, n_ctx)),
            dma((2, chunks, n_ctx)), dma((2, chunks, n_ctx)),
            dma((n_dp,)), dma((n_dp,)), dma((n_dp,)), dma((n_dp,)),
            dma((n_ctx,)), dma((n_ctx,)),
        ],
        compiler_params=pltpu.CompilerParams(
            vmem_limit_bytes=48 * 1024 * 1024, collective_id=0, has_side_effects=True),
        name="hyena",
    )(tokens, embedding, cotangent, long_filter, short_filter)


def solution(mesh):
    in_specs = (P("dp", "ctx"), P(), P("dp", "ctx", None), P("ctx", None), P())
    out_specs = (P("dp", "ctx", None), P("dp", "ctx", None), P("ctx", None), P())
    return jax.shard_map(
        on_device, mesh=mesh, in_specs=in_specs, out_specs=out_specs, check_vma=False
    )
```

time: 171 us -> 60 us (0.35)
  blocking collectives: 62.6 us -> 0 us
  local copies, waits for them, and re-layouts: 27.1 us -> 7.94 us
  Pallas kernels: 36.2 us -> 51.1 us
  between operations: 14.2 us -> 0.65 us
  other arithmetic: 12.4 us -> 0 us
  waiting for transfers between devices: 10.1 us -> 0 us
  starting transfers between devices: 7.9 us -> 0 us
    psum x1 -> x0, blocking collectives: 41.8 us -> none  [on_device(): short_sum = lax.psum(short_part, 'dp')]
    all_gather x2 -> x0, blocking collectives: 20.9 us -> none  [the longest x1 11.4 us: on_device(): grad_short = lax.all_gather(short_sum, 'ctx', axis=1, tiled=True)]
    pallas_call x1, Pallas kernels: 36.2 us -> 51.1 us  [on_device(): pl.pallas_call(kernel, out_shape=[jax.ShapeDtypeStruct(cotangent.shape, B...]
    unnamed x1 -> x0, other arithmetic: 12.3 us -> none
    slice x5 -> x0, local copies, waits for them, and re-layouts: 9.6 us -> none  [the longest x3 5.93 us: on_device(): both[1:2]]
    psum x1 -> x0, waiting for transfers between devices: 9.38 us -> none  [on_device(): grad_long = lax.psum(long_part, 'dp')]
    all_to_all x2 -> x0, starting transfers between devices: 7.85 us -> none  [the longest x1 4.21 us: on_device(): lax.all_to_all(cotangent, 'ctx', split_axis=2, concat_axis=1, tiled=True)[0]]
    unnamed x21 -> x14, local copies, waits for them, and re-layouts: 11.1 us -> 7.94 us
  transfers between devices with their start and end apart: 3 -> 0, of which waited for: 1 -> 0; matrix products, arithmetic and copies ran while one was open for 8% -> 0% of each run, Pallas kernels for 0% -> 0%
where the time goes in v1:
time: 60 us; the launch traced here: 59.7 us
  Pallas kernels  51.1 us (85%)
  local copies, waits for them, and re-layouts  7.94 us (13%)
  between operations  0.65 us (1%)
    pallas_call x1, Pallas kernels, on_device(): pl.pallas_call(kernel, out_shape=[jax.ShapeDtypeStruct(cotangent.shape, B...  51.1 us
    unnamed x14, local copies, waits for them, and re-layouts  7.94 us

profile of v1, /device:TPU:0, one launch (start us, length us, event | category | flops | bytes accessed | tf_op | source)
XLA Modules:
  0.0 59.7 jit_solution(2051057154577217679)
XLA Ops:
  0.6 0.0 copy-start
  0.6 1.6 %copy-done = bf16[512,2048]{1,0:T(8,128)(2,1)S(1)} copy-done((bf16[512,2048]{1,0:T(8,128)(2,1)S(1)}, bf16[512,2048]{1,0:T(8,128)(2,1)}, u32[]{:S(2)}) %copy-start) | copy-done | bytes 2097176
  2.2 0.0 copy-start.1
  2.2 1.0 %copy-done.1 = bf16[1,128,2048]{2,1,0:T(8,128)(2,1)S(1)} copy-done((bf16[1,128,2048]{2,1,0:T(8,128)(2,1)S(1)}, bf16[1,128,2048]{2,1,0:T(8,128)(2,1)}, u32[]{:S(2)}) %copy-start.1) | copy-done | bytes 524312
  3.3 0.0 copy-start.2
  3.3 0.9 %copy-done.2 = f32[3,7,2048]{2,1,0:T(8,128)S(1)} copy-done((f32[3,7,2048]{2,1,0:T(8,128)S(1)}, f32[3,7,2048]{2,1,0:T(8,128)}, u32[]{:S(2)}) %copy-start.2) | copy-done | bytes 172056
  4.2 0.0 copy-start.3
  4.2 0.8 %copy-done.3 = f32[32,512]{1,0:T(8,128)S(1)} copy-done((f32[32,512]{1,0:T(8,128)S(1)}, f32[32,512]{1,0:T(8,128)}, u32[]{:S(2)}) %copy-start.3) | copy-done | bytes 65560
  5.0 0.0 copy-start.4
  5.0 0.7 %copy-done.4 = s32[1,128]{1,0:T(1,128)S(1)} copy-done((s32[1,128]{1,0:T(1,128)S(1)}, s32[1,128]{1,0:T(1,128)}, u32[]{:S(2)}) %copy-start.4) | copy-done | bytes 536
  5.7 51.1 %hyena.1 = (bf16[1,128,2048]{2,1,0:T(8,128)(2,1)S(1)}, bf16[1,128,2048]{2,1,0:T(8,128)(2,1)S(1)}, f32[32,512]{1,0:T(8,128)S(1)}, f32[3,7,2048]{2,1,0:T(8,128)S(1)}) custom-call(s32[1,128]{1,0:T(1,128)S(1)} %copy-done.4, bf16[512,2048]{1,0:T(8,128)(2,1)S(1)} %copy-done, bf16[1,128,2048]{2,1,0:T(8,128)(2,1)S(1)} %copy-done.1, f32[32,512]{1,0:T(8,128)S(1)} %copy-done.3, ...), custom_call_target="tpu_custom_call" | custom-call | tf_op jit(solution)/shard_map/hyena/pallas_call | solution.py:314
  56.8 0.8 %copy.13 = bf16[1,128,2048]{2,1,0:T(8,128)(2,1)} copy(bf16[1,128,2048]{2,1,0:T(8,128)(2,1)S(1)} %get-tuple-element.8) | data formatting | bytes 1048576
  57.6 0.8 %copy.14 = bf16[1,128,2048]{2,1,0:T(8,128)(2,1)} copy(bf16[1,128,2048]{2,1,0:T(8,128)(2,1)S(1)} %get-tuple-element.9) | data formatting | bytes 1048576
  58.4 0.6 %copy.15 = f32[32,512]{1,0:T(8,128)} copy(f32[32,512]{1,0:T(8,128)S(1)} %get-tuple-element.10) | data formatting | bytes 131072
  59.0 0.7 %copy.16 = f32[3,7,2048]{2,1,0:T(8,128)} copy(f32[3,7,2048]{2,1,0:T(8,128)S(1)} %get-tuple-element.11) | data formatting | bytes 344064
Async XLA Ops:
  0.6 1.6 %copy-start = (bf16[512,2048]{1,0:T(8,128)(2,1)S(1)}, bf16[512,2048]{1,0:T(8,128)(2,1)}, u32[]{:S(2)}) copy-start(bf16[512,2048]{1,0:T(8,128)(2,1)} %emb_ref.1) | copy-start | bytes 6291460
  2.2 1.0 %copy-start.1 = (bf16[1,128,2048]{2,1,0:T(8,128)(2,1)S(1)}, bf16[1,128,2048]{2,1,0:T(8,128)(2,1)}, u32[]{:S(2)}) copy-start(bf16[1,128,2048]{2,1,0:T(8,128)(2,1)} %cot_ref.1) | copy-start | bytes 1572868
  3.3 0.9 %copy-start.2 = (f32[3,7,2048]{2,1,0:T(8,128)S(1)}, f32[3,7,2048]{2,1,0:T(8,128)}, u32[]{:S(2)}) copy-start(f32[3,7,2048]{2,1,0:T(8,128)} %w_ref.1) | copy-start | bytes 516100
  4.2 0.8 %copy-start.3 = (f32[32,512]{1,0:T(8,128)S(1)}, f32[32,512]{1,0:T(8,128)}, u32[]{:S(2)}) copy-start(f32[32,512]{1,0:T(8,128)} %h_ref.1) | copy-start | bytes 196612
  5.0 0.7 %copy-start.4 = (s32[1,128]{1,0:T(1,128)S(1)}, s32[1,128]{1,0:T(1,128)}, u32[]{:S(2)}) copy-start(s32[1,128]{1,0:T(1,128)} %tok_ref.1) | copy-start | bytes 1540

commit v2 on v1

--- a/solution.py
+++ b/solution.py
@@ -6,6 +6,7 @@
 from jax.sharding import PartitionSpec as P
 
 LANES = 128
+VMEM_LIMIT = 63 * 1024 * 1024
 F32 = jnp.float32
 BF16 = jnp.bfloat16
 MESH = pl.DeviceIdType.MESH
@@ -15,11 +16,11 @@
     return lax.dot_general(a, b, (((da,), (db,)), ((), ())), preferred_element_type=F32)
 
 
-def kernel(tok_ref, emb_ref, cot_ref, h_ref, w_ref,
+def kernel(tok_ref, emb_ref, cot_ref, h_in, w_in,
            blk_ref, gin_ref, long_ref, short_ref,
            ids, emb, cot_b, hot, e_t, cot_t, blk_t, gin_t, w_s, w_t, blk_s, gin_s,
-           long_s, short_t, red, got, summed, short_b,
-           emb_sem, own_sem, out_sem, tok_send, tok_recv, cot_send, cot_recv,
+           long_s, short_t, red, got, summed, short_b, h_ref, w_ref,
+           emb_sem, in_sem, own_sem, out_sem, tok_send, tok_recv, cot_send, cot_recv,
            res_send, res_recv, red_send, red_recv, sum_send, sum_recv, sh_send, sh_recv):
     n_ctx, n_dp = lax.axis_size("ctx"), lax.axis_size("dp")
     me, mine = lax.axis_index("ctx"), lax.axis_index("dp")
@@ -31,7 +32,7 @@
     own_len = tok_ref.shape[1]
     chunks = chans // LANES
     scale = 1.0 / (n_dp * group)
-    per = got.shape[1]
+    per = got.shape[2]
     where = pl.ds(pl.multiple_of(me * chans, chans), chans)
 
     def ctx(k):
@@ -47,6 +48,11 @@
 
     emb_copy = pltpu.make_async_copy(emb_ref.at[:, where], emb, emb_sem)
     emb_copy.start()
+    loads = [pltpu.make_async_copy(h_in, h_ref, in_sem.at[0]),
+             pltpu.make_async_copy(w_in.at[:, :, where], w_ref, in_sem.at[1]),
+             pltpu.make_async_copy(tok_ref, ids.at[me], in_sem.at[2])]
+    for copy in loads:
+        copy.start()
 
     def cot_part(p, c):
         return cot_ref.at[0, :, pl.ds(pl.multiple_of(p * chans + c * LANES, LANES), LANES)]
@@ -79,14 +85,15 @@
     for c in range(chunks):
         for k in range(1, n_ctx):
             cot_copy(k, c, me).start()
-    ids[me] = tok_ref[...]
+    for copy in loads:
+        copy.wait()
 
     w_s[...] = jnp.zeros_like(w_s)
     for s in range(3):
-        w_s[s * 8:s * 8 + taps, :] = w_ref[s, :, where]
+        w_s[s * 8:s * 8 + taps, :] = w_ref[s, :, :]
     for c in range(chunks):
         w_t[c * LANES:(c + 1) * LANES, :] = w_s[:, c * LANES:(c + 1) * LANES].T
-    if red.shape[0] > (groups // 8) * n + 3 * chunks:
+    if red.shape[1] > n + 3:
         red[...] = jnp.zeros_like(red)
 
     for k in range(1, n_ctx):
@@ -202,6 +209,48 @@
         return [pltpu.make_async_copy(src.at[c, me], dst.at[0, :, at], out_sem.at[i, c])
                 for i, (src, dst) in enumerate(((blk_s, blk_ref), (gin_s, gin_ref)))]
 
+    def part_copy(c, k, slot):
+        return remote(red.at[c, pl.ds(dp(k) * per, per)], got.at[c, slot],
+                      red_send.at[c, k], red_recv.at[c, k], {"dp": dp(k)})
+
+    def sum_copy(c, k, slot):
+        return remote(summed.at[c, mine], summed.at[c, slot],
+                      sum_send.at[c, k], sum_recv.at[c, k], {"dp": dp(k)})
+
+    def short_copy(c, k, slot):
+        return remote(short_b.at[c, me], short_b.at[c, slot],
+                      sh_send.at[c, k], sh_recv.at[c, k], {"ctx": ctx(k)})
+
+    def scatter(c):
+        cs = pl.ds(pl.multiple_of(c * LANES, LANES), LANES)
+        gs = pl.ds(pl.multiple_of(c * in_chunk, in_chunk), in_chunk)
+        for i in range(n):
+            red[c, i] = long_s[gs, i * LANES:(i + 1) * LANES]
+        turned = short_t[cs, :].T
+        for r in range(3):
+            red[c, n + r] = turned[r * 8:(r + 1) * 8, :]
+        for k in range(1, n_dp):
+            part_copy(c, k, mine).start()
+        got[c, mine] = red[c, pl.ds(mine * per, per)]
+
+    def reduce(c):
+        for k in range(1, n_dp):
+            part_copy(c, k, dp(n_dp - k)).wait()
+        total = got[c, 0]
+        for i in range(1, n_dp):
+            total = total + got[c, i]
+        summed[c, mine] = total
+        for k in range(1, n_dp):
+            sum_copy(c, k, mine).start()
+
+    def finish(c):
+        for k in range(1, n_dp):
+            sum_copy(c, k, dp(n_dp - k)).wait()
+        for r in range(3):
+            short_b[c, me, r] = summed[c, (n + r) // per, (n + r) % per]
+        for k in range(1, n_ctx):
+            short_copy(c, k, me).start()
+
     in_chunk = LANES // group
     step = 2 if in_chunk % 2 == 0 else 1
 
@@ -223,6 +272,7 @@
             for g, r, z in zip(gs, a, m):
                 third(g, *r[:7], *z)
 
+        scatter(c)
         for i in range(n_ctx):
             blk_s[c, i] = blk_t[cs, i * own_len:(i + 1) * own_len].T.astype(BF16)
             gin_s[c, i] = gin_t[cs, i * own_len:(i + 1) * own_len].T.astype(BF16)
@@ -232,61 +282,28 @@
         for copy in own_results(c):
             copy.start()
 
-    t = 0
-    for r in range(groups // 8):
+        @pl.when(c > 0)
+        def _():
+            reduce(c - 1)
+
+        @pl.when(c > 1)
+        def _():
+            finish(c - 2)
+
+    reduce(chunks - 1)
+    for c in range(max(chunks - 2, 0), chunks):
+        finish(c)
+    for c in range(chunks):
         for i in range(n):
-            red[t] = long_s[r * 8:(r + 1) * 8, i * LANES:(i + 1) * LANES]
-            t += 1
-    for c in range(chunks):
-        turned = short_t[c * LANES:(c + 1) * LANES, :].T
-        for r in range(3):
-            red[t] = turned[r * 8:(r + 1) * 8, :]
-            t += 1
-
-    def part_copy(k, slot):
-        return remote(red.at[pl.ds(dp(k) * per, per)], got.at[slot],
-                      red_send.at[k], red_recv.at[k], {"dp": dp(k)})
-
-    def sum_copy(k, slot):
-        return remote(summed.at[mine], summed.at[slot],
-                      sum_send.at[k], sum_recv.at[k], {"dp": dp(k)})
-
-    for k in range(1, n_dp):
-        part_copy(k, mine).start()
-    got[mine] = red[pl.ds(mine * per, per)]
-    for k in range(1, n_dp):
-        part_copy(k, dp(n_dp - k)).wait()
-    total = got[0]
-    for i in range(1, n_dp):
-        total = total + got[i]
-    summed[mine] = total
-    for k in range(1, n_dp):
-        sum_copy(k, mine).start()
-    for k in range(1, n_dp):
-        sum_copy(k, dp(n_dp - k)).wait()
-
-    base_t = (groups // 8) * n
-    for c in range(chunks):
-        for r in range(3):
-            t = base_t + c * 3 + r
-            short_b[me, r, :, c * LANES:(c + 1) * LANES] = summed[t // per, t % per]
-
-    def short_copy(k, slot):
-        return remote(short_b.at[me], short_b.at[slot],
-                      sh_send.at[k], sh_recv.at[k], {"ctx": ctx(k)})
-
-    for k in range(1, n_ctx):
-        short_copy(k, me).start()
-    t = 0
-    for r in range(groups // 8):
-        for i in range(n):
-            long_ref[r * 8:(r + 1) * 8, i * LANES:(i + 1) * LANES] = summed[t // per, t % per]
-            t += 1
-    for k in range(1, n_ctx):
-        short_copy(k, ctx(n_ctx - k)).wait()
-    for i in range(n_ctx):
-        for s in range(3):
-            short_ref[s, :, i * chans:(i + 1) * chans] = short_b[i, s, :taps, :]
+            long_ref[c * in_chunk:(c + 1) * in_chunk, i * LANES:(i + 1) * LANES] = (
+                summed[c, i // per, i % per])
+    for c in range(chunks):
+        for k in range(1, n_ctx):
+            short_copy(c, k, ctx(n_ctx - k)).wait()
+        for i in range(n_ctx):
+            for s in range(3):
+                at = i * chans + c * LANES
+                short_ref[s, :, at:at + LANES] = short_b[c, i, s, :taps, :]
 
     @pl.loop(0, chunks)
     def _(c):
@@ -295,6 +312,15 @@
                 copy.wait()
         for copy in own_results(c):
             copy.wait()
+
+
+def hand_over(*refs):
+    sems = refs[8]
+    copies = [pltpu.make_async_copy(refs[i], refs[4 + i], sems.at[i]) for i in range(4)]
+    for copy in copies:
+        copy.start()
+    for copy in copies:
+        copy.wait()
 
 
 def on_device(tokens, embedding, cotangent, long_filter, short_filter):
@@ -306,12 +332,11 @@
     groups, length = long_filter.shape
     own_len = cotangent.shape[1]
     chunks = chans // LANES
-    tiles = (groups // 8) * (length // LANES) + streams * chunks
-    per = -(-tiles // n_dp)
+    per = -(-(length // LANES + streams) // n_dp)
     vmem = pl.BlockSpec(memory_space=pltpu.VMEM)
-    hbm = pl.BlockSpec(memory_space=pl.ANY)
+    hbm = pl.BlockSpec(memory_space=pltpu.HBM)
     dma = pltpu.SemaphoreType.DMA
-    return pl.pallas_call(
+    parts = pl.pallas_call(
         kernel,
         out_shape=[
             jax.ShapeDtypeStruct(cotangent.shape, BF16),
@@ -319,7 +344,7 @@
             jax.ShapeDtypeStruct((groups, length), F32),
             jax.ShapeDtypeStruct(short_filter.shape, F32),
         ],
-        in_specs=[vmem, hbm, hbm, vmem, vmem],
+        in_specs=[hbm] * 5,
         out_specs=[hbm, hbm, vmem, vmem],
         scratch_shapes=[
             pltpu.VMEM((n_ctx, 1, own_len), jnp.int32),
@@ -336,21 +361,33 @@
             pltpu.VMEM((chunks, n_ctx, own_len, LANES), BF16),
             pltpu.VMEM((groups, length), F32),
             pltpu.VMEM((chans, LANES), F32),
-            pltpu.VMEM((per * n_dp, 8, LANES), F32),
-            pltpu.VMEM((n_dp, per, 8, LANES), F32),
-            pltpu.VMEM((n_dp, per, 8, LANES), F32),
-            pltpu.VMEM((n_ctx, streams, 8, chans), F32),
-            dma, dma((chunks,)), dma((2, chunks)),
+            pltpu.VMEM((chunks, per * n_dp, 8, LANES), F32),
+            pltpu.VMEM((chunks, n_dp, per, 8, LANES), F32),
+            pltpu.VMEM((chunks, n_dp, per, 8, LANES), F32),
+            pltpu.VMEM((chunks, n_ctx, streams, 8, LANES), F32),
+            pltpu.VMEM((groups, length), F32),
+            pltpu.VMEM((streams, taps, chans), F32),
+            dma, dma((3,)), dma((chunks,)), dma((2, chunks)),
             dma((n_ctx,)), dma((n_ctx,)),
             dma((chunks, n_ctx)), dma((chunks, n_ctx)),
             dma((2, chunks, n_ctx)), dma((2, chunks, n_ctx)),
-            dma((n_dp,)), dma((n_dp,)), dma((n_dp,)), dma((n_dp,)),
-            dma((n_ctx,)), dma((n_ctx,)),
+            dma((chunks, n_dp)), dma((chunks, n_dp)), dma((chunks, n_dp)), dma((chunks, n_dp)),
+            dma((chunks, n_ctx)), dma((chunks, n_ctx)),
         ],
         compiler_params=pltpu.CompilerParams(
-            vmem_limit_bytes=48 * 1024 * 1024, collective_id=0, has_side_effects=True),
+            vmem_limit_bytes=VMEM_LIMIT, collective_id=0, has_side_effects=True),
         name="hyena",
     )(tokens, embedding, cotangent, long_filter, short_filter)
+    anywhere = pl.BlockSpec(memory_space=pl.ANY)
+    return pl.pallas_call(
+        hand_over,
+        out_shape=[jax.ShapeDtypeStruct(p.shape, p.dtype) for p in parts],
+        in_specs=[anywhere] * 4,
+        out_specs=[anywhere] * 4,
+        scratch_shapes=[dma((4,))],
+        compiler_params=pltpu.CompilerParams(vmem_limit_bytes=VMEM_LIMIT),
+        name="hand_over",
+    )(*parts)
 
 
 def solution(mesh):

time: 60 us -> 92.6 us (1.54)
  Pallas kernels: 51.1 us -> 91.8 us
  local copies, waits for them, and re-layouts: 7.94 us -> 0 us
    pallas_call x0 -> x1, Pallas kernels: none -> 40.8 us  [on_device(): pl.pallas_call(hand_over, out_shape=[jax.ShapeDtypeStruct(p.shape, p.dtyp...]
    unnamed x14 -> x0, local copies, waits for them, and re-layouts: 7.94 us -> none
where the time goes in v2:
time: 92.6 us; the launch traced here: 92.4 us
  Pallas kernels  91.8 us (99%)
    pallas_call x1, Pallas kernels, on_device(): pl.pallas_call(kernel, out_shape=[jax.ShapeDtypeStruct(cotangent.shape, B...  50.9 us
    pallas_call x1, Pallas kernels, on_device(): pl.pallas_call(hand_over, out_shape=[jax.ShapeDtypeStruct(p.shape, p.dtyp...  40.8 us

profile of v2, /device:TPU:0, one launch (start us, length us, event | category | flops | bytes accessed | tf_op | source)
XLA Modules:
  0.0 92.4 jit_solution(17027086916126157235)
XLA Ops:
  0.6 50.9 %hyena.1 = (bf16[1,128,2048]{2,1,0:T(8,128)(2,1)}, bf16[1,128,2048]{2,1,0:T(8,128)(2,1)}, f32[32,512]{1,0:T(8,128)}, f32[3,7,2048]{2,1,0:T(8,128)}) custom-call(s32[1,128]{1,0:T(1,128)} %tok_ref.1, bf16[512,2048]{1,0:T(8,128)(2,1)} %emb_ref.1, bf16[1,128,2048]{2,1,0:T(8,128)(2,1)} %cot_ref.1, f32[32,512]{1,0:T(8,128)} %h_in.1, f32[3,7,2048]{2,1,0:T(8,128)} %w_in.1), custom_call_target="tpu_custom_call" | custom-call | tf_op jit(solution)/shard_map/hyena/pallas_call | solution.py:339
  51.6 40.8 %hand_over.1 = (bf16[1,128,2048]{2,1,0:T(8,128)(2,1)}, bf16[1,128,2048]{2,1,0:T(8,128)(2,1)}, f32[32,512]{1,0:T(8,128)}, f32[3,7,2048]{2,1,0:T(8,128)}) custom-call(bf16[1,128,2048]{2,1,0:T(8,128)(2,1)} %get-tuple-element.8.refs_0_, bf16[1,128,2048]{2,1,0:T(8,128)(2,1)} %get-tuple-element.9.refs_1_, f32[32,512]{1,0:T(8,128)} %get-tuple-element.10.refs_2_, ...), custom_call_target="tpu_custom_call" | custom-call | tf_op jit(solution)/shard_map/hand_over/pallas_call | solution.py:382

commit v3 on v2

--- a/solution.py
+++ b/solution.py
@@ -312,15 +312,6 @@
                 copy.wait()
         for copy in own_results(c):
             copy.wait()
-
-
-def hand_over(*refs):
-    sems = refs[8]
-    copies = [pltpu.make_async_copy(refs[i], refs[4 + i], sems.at[i]) for i in range(4)]
-    for copy in copies:
-        copy.start()
-    for copy in copies:
-        copy.wait()
 
 
 def on_device(tokens, embedding, cotangent, long_filter, short_filter):
@@ -378,16 +369,7 @@
             vmem_limit_bytes=VMEM_LIMIT, collective_id=0, has_side_effects=True),
         name="hyena",
     )(tokens, embedding, cotangent, long_filter, short_filter)
-    anywhere = pl.BlockSpec(memory_space=pl.ANY)
-    return pl.pallas_call(
-        hand_over,
-        out_shape=[jax.ShapeDtypeStruct(p.shape, p.dtype) for p in parts],
-        in_specs=[anywhere] * 4,
-        out_specs=[anywhere] * 4,
-        scratch_shapes=[dma((4,))],
-        compiler_params=pltpu.CompilerParams(vmem_limit_bytes=VMEM_LIMIT),
-        name="hand_over",
-    )(*parts)
+    return tuple(parts)
 
 
 def solution(mesh):

time: 92.6 us -> 56.9 us (0.61)
  Pallas kernels: 91.8 us -> 50.9 us
  local copies, waits for them, and re-layouts: 0 us -> 5.12 us
    pallas_call x1 -> x0, Pallas kernels: 40.8 us -> none  [on_device(): pl.pallas_call(hand_over, out_shape=[jax.ShapeDtypeStruct(p.shape, p.dtyp...]
    unnamed x0 -> x8, local copies, waits for them, and re-layouts: none -> 5.12 us
where the time goes in v3:
time: 56.9 us; the launch traced here: 56.7 us
  Pallas kernels  50.9 us (89%)
  local copies, waits for them, and re-layouts  5.12 us (9%)
  between operations  0.66 us (1%)
    pallas_call x1, Pallas kernels, on_device(): pl.pallas_call(kernel, out_shape=[jax.ShapeDtypeStruct(cotangent.shape, B...  50.9 us
    unnamed x8, local copies, waits for them, and re-layouts  5.12 us

profile of v3, /device:TPU:0, one launch (start us, length us, event | category | flops | bytes accessed | tf_op | source)
XLA Modules:
  0.0 56.7 jit_solution(15000684765383118368)
XLA Ops:
  0.6 50.9 %hyena.1 = (bf16[1,128,2048]{2,1,0:T(8,128)(2,1)}, bf16[1,128,2048]{2,1,0:T(8,128)(2,1)}, f32[32,512]{1,0:T(8,128)}, f32[3,7,2048]{2,1,0:T(8,128)}) custom-call(s32[1,128]{1,0:T(1,128)} %tok_ref.1, bf16[512,2048]{1,0:T(8,128)(2,1)} %emb_ref.1, bf16[1,128,2048]{2,1,0:T(8,128)(2,1)} %cot_ref.1, f32[32,512]{1,0:T(8,128)} %h_in.1, f32[3,7,2048]{2,1,0:T(8,128)} %w_in.1), custom_call_target="tpu_custom_call" | custom-call | tf_op jit(solution)/shard_map/hyena/pallas_call | solution.py:330
  51.6 0.0 copy-start.1
  51.6 0.0 copy-start
  51.6 1.9 %copy.13 = bf16[1,128,2048]{2,1,0:T(8,128)(2,1)} copy(bf16[1,128,2048]{2,1,0:T(8,128)(2,1)} %get-tuple-element.8) | data formatting | bytes 1048576
  53.5 1.9 %copy.14 = bf16[1,128,2048]{2,1,0:T(8,128)(2,1)} copy(bf16[1,128,2048]{2,1,0:T(8,128)(2,1)} %get-tuple-element.9) | data formatting | bytes 1048576
  55.4 0.0 copy-done.1
  55.4 0.6 %copy.15 = f32[32,512]{1,0:T(8,128)} copy(f32[32,512]{1,0:T(8,128)S(1)} %copy-done.1) | data formatting | bytes 131072
  56.0 0.0 copy-done
  56.0 0.7 %copy.16 = f32[3,7,2048]{2,1,0:T(8,128)} copy(f32[3,7,2048]{2,1,0:T(8,128)S(1)} %copy-done) | data formatting | bytes 344064
Async XLA Ops:
  51.6 3.8 %copy-start.1 = (f32[32,512]{1,0:T(8,128)S(1)}, f32[32,512]{1,0:T(8,128)}, u32[]{:S(2)}) copy-start(f32[32,512]{1,0:T(8,128)} %get-tuple-element.10) | copy-start | bytes 196612
  51.6 4.4 %copy-start = (f32[3,7,2048]{2,1,0:T(8,128)S(1)}, f32[3,7,2048]{2,1,0:T(8,128)}, u32[]{:S(2)}) copy-start(f32[3,7,2048]{2,1,0:T(8,128)} %get-tuple-element.11) | copy-start | bytes 516100
